TPU v7x, 32 devices: a whole 2x2x4 slice. The times are simulated.
32 devices in a mesh: groups: 2 (over y), batch: 4 (over z), tensor: 4 (over x, core).
Axes of the slice: x: 2, y: 2, z: 4, core: 2. Of those that a mesh axis runs over, the one named last changes fastest.
Arguments:
- queries: bfloat16 [768, 8192], P(('groups', 'batch'), 'tensor'), parts along dimension 0, may hold values from -88 to 88, as said below
- cached_keys: bfloat16 [768, 64, 1024], P(('groups', 'batch'), None, 'tensor'), parts along dimension 0, may hold values from -4 to 4, as said below
- cached_values: bfloat16 [768, 64, 1024], P(('groups', 'batch'), None, 'tensor'), parts along dimension 0, may hold values from -5 to 5
- token_key: bfloat16 [768, 1024], P(('groups', 'batch'), 'tensor'), parts along dimension 0, may hold values from -5 to 5
- token_value: bfloat16 [768, 1024], P(('groups', 'batch'), 'tensor'), parts along dimension 0, may hold values from -5 to 5
- lengths: int32 [768], P(('groups', 'batch')), parts along dimension 0, may hold values from 2 to 64
- adapter_index: int32 [768], P(('groups', 'batch')), parts along dimension 0, may hold values from 0 to 15, as said below
- output_weight: bfloat16 [8192, 8192], P('tensor', 'batch'), may hold values from -0.0625 to 0.0625
- adapter_down: bfloat16 [16, 8192, 64], P('batch', 'tensor'), may hold values from -0.0625 to 0.0625
- adapter_up: bfloat16 [16, 64, 8192], P('batch', None, 'tensor'), may hold values from -0.75 to 0.75
Outputs:
- projected: bfloat16 [768, 8192], P(('groups', 'batch'), 'tensor'), parts along dimension 0
There are 2 independent parts, one for each index of `groups`. A program takes and returns all parts, laid end to end along the dimension named above; an argument that names none is the same for every part. Nothing has to cross between parts.
Inputs may be any that keep to these rules, and one draw needn't show every extreme that they name: `queries`: entries of order one; in some requests every head's query is a multiple of 10 to 22 of the request's first cached key of that head's key-value head. `cached_keys`: the second cached key of each request is 0.99 times its first. `adapter_index`: device blocks are the aligned runs of 96 requests; owner o holds adapters 4 * o to 4 * o + 3. No block has more than 48 requests on adapters of one owner, and in every draw some owner receives exactly 48 from every block.
All inputs are finite; a program needn't handle non-finite values.
Results may differ from a plain program's by a relative error of at most 0.0057.
Values may be sent and summed in bfloat16 or wider, within the bound.
A program may use at most 64 MiB of HBM per device.

v0:
```python
import jax
import jax.numpy as jnp
from jax import lax
from jax.sharding import PartitionSpec as P

HEAD_SIZE = 128


adapter_scale = 0.25


def finish_output(
    flattened_rows, select_adapter, adapter_down, adapter_up, owner_count, taken_rows
):
    down_factor = jnp.einsum(
        "tj,ojx->tox", flattened_rows, adapter_down, preferred_element_type=jnp.float32
    )
    partial_small = jnp.einsum("sak,sa->sk", down_factor, select_adapter)
    small_product = lax.psum(partial_small, "tensor").astype(jnp.bfloat16)
    up_factor = jnp.einsum(
        "yg,rgo->yro", small_product, adapter_up, preferred_element_type=jnp.float32
    )
    final_result = (adapter_scale * jnp.einsum("czp,cz->cp", up_factor, select_adapter)).astype(
        jnp.bfloat16
    )
    final_result = final_result.reshape(owner_count, taken_rows, final_result.shape[1])
    return lax.all_to_all(final_result, "batch", split_axis=0, concat_axis=0, tiled=True)


def body(
    queries,
    cached_keys,
    cached_values,
    token_key,
    token_value,
    lengths,
    adapter_index,
    output_weight,
    adapter_down,
    adapter_up,
):
    rows = queries.shape[0]
    width = queries.shape[1]
    span = cached_keys.shape[1]
    kv_local = cached_keys.shape[2] // HEAD_SIZE
    group = width // HEAD_SIZE // kv_local
    score_scale = HEAD_SIZE ** (-0.5)
    query_rows = queries.reshape(rows, kv_local, group, HEAD_SIZE)
    keys = cached_keys.reshape(rows, span, kv_local, HEAD_SIZE)
    values = cached_values.reshape(rows, span, kv_local, HEAD_SIZE)
    newest_key = token_key.reshape(rows, kv_local, HEAD_SIZE)
    fresh_value = token_value.reshape(rows, kv_local, HEAD_SIZE)
    scores = (
        jnp.einsum("rkgd,rlkd->rkgl", query_rows, keys, preferred_element_type=jnp.float32)
        * score_scale
    )
    owned_rows = (
        jnp.einsum("rkgd,rkd->rkg", query_rows, newest_key, preferred_element_type=jnp.float32)
        * score_scale
    )
    valid = lax.broadcasted_iota(jnp.int32, (rows, span), 1) < lengths[:, None]
    scores = jnp.where(valid[:, None, None, :], scores, -jnp.inf)
    top = jnp.maximum(jnp.max(scores, axis=-1), owned_rows)
    expo = jnp.exp(scores - top[..., None])
    own_expo = jnp.exp(owned_rows - top)
    total = jnp.sum(expo, axis=-1) + own_expo
    weights = (expo / total[..., None]).astype(jnp.bfloat16)
    own_weight = (own_expo / total).astype(jnp.bfloat16)
    mixed = jnp.einsum("rkgl,rlkd->rkgd", weights, values, preferred_element_type=jnp.float32)
    mixed = (
        mixed
        + own_weight.astype(jnp.float32)[..., None] * fresh_value.astype(jnp.float32)[:, :, None, :]
    )
    attention_output = mixed.reshape(rows, width).astype(jnp.bfloat16)
    owner_count = lax.axis_size("batch")
    held_rows = adapter_down.shape[0]
    slots = max(2, 2 * rows // owner_count)
    table = owner_count * slots
    partial_sums = jnp.dot(
        lax.all_gather(attention_output, "batch", axis=0, tiled=True),
        output_weight,
        preferred_element_type=jnp.float32,
    )
    routed = lax.all_to_all(partial_sums, "batch", split_axis=0, concat_axis=1, tiled=True)
    base_output = lax.psum_scatter(routed, "tensor", scatter_dimension=1, tiled=True)
    owner = adapter_index // held_rows
    local = adapter_index % held_rows
    owner_hot = (owner[:, None] == lax.broadcasted_iota(jnp.int32, (rows, owner_count), 1)).astype(
        jnp.bfloat16
    )
    earlier = (
        lax.broadcasted_iota(jnp.int32, (rows, rows), 0)
        > lax.broadcasted_iota(jnp.int32, (rows, rows), 1)
    ).astype(jnp.bfloat16)
    before = jnp.dot(earlier, owner_hot, preferred_element_type=jnp.float32)
    position = jnp.sum(before * owner_hot.astype(jnp.float32), axis=1).astype(jnp.int32)
    target = owner * slots + position
    place_rows = (target[:, None] == lax.broadcasted_iota(jnp.int32, (rows, table), 1)).astype(
        jnp.bfloat16
    )
    send_rows = jnp.einsum(
        "rs,rf->sf", place_rows, attention_output, preferred_element_type=jnp.float32
    ).astype(jnp.bfloat16)
    marked = jnp.where(place_rows > 0, (local[:, None] + 1).astype(jnp.float32), 0.0)
    send_ids = (jnp.max(marked, axis=0) - 1.0).astype(jnp.bfloat16)
    send_rows = send_rows.reshape(owner_count, slots, width)
    send_ids = send_ids.reshape(owner_count, slots)
    incoming = lax.all_to_all(send_rows, "batch", split_axis=0, concat_axis=0, tiled=True)
    tags = lax.all_to_all(send_ids, "batch", split_axis=0, concat_axis=0, tiled=True)
    taken_rows = incoming.shape[1]
    flattened_rows = incoming.reshape(-1, width)
    flat_tags = tags.reshape(-1).astype(jnp.float32)
    select_local = (
        flat_tags[:, None]
        == lax.broadcasted_iota(jnp.float32, (flattened_rows.shape[0], held_rows), 1)
    ).astype(jnp.float32)
    returned_output = finish_output(
        flattened_rows, select_local, adapter_down, adapter_up, owner_count, taken_rows
    )
    returned_output = returned_output.reshape(table, -1)
    adapter_rows = jnp.dot(place_rows, returned_output, preferred_element_type=jnp.float32)
    return (base_output + adapter_rows).astype(jnp.bfloat16)


def solution(mesh):
    placed = (
        P(("groups", "batch"), "tensor"),
        P(("groups", "batch"), None, "tensor"),
        P(("groups", "batch"), None, "tensor"),
        P(("groups", "batch"), "tensor"),
        P(("groups", "batch"), "tensor"),
        P(("groups", "batch")),
        P(("groups", "batch")),
        P("tensor", "batch"),
        P("batch", "tensor", None),
        P("batch", None, "tensor"),
    )
    return jax.shard_map(
        body,
        mesh=mesh,
        in_specs=placed,
        out_specs=P(("groups", "batch"), "tensor"),
        check_vma=False,
    )
```

profile of v0, /device:TPU:0, one launch (start us, length us, event | category | flops | bytes accessed | tf_op | source)
XLA Modules:
  0.0 233.1 jit_solution(492201552238004437)
XLA Ops:
  6.5 1.5 iota_compare_fusion.5
  8.0 1.5 reshape.109
  9.5 1.5 reshape.97
  11.0 1.1 copy.56
  12.0 1.9 fusion.43
  13.9 0.9 copy.42
  14.8 5.2 %fusion.42 = (f32[96,2,8]{2,1,0:T(2,128)}, f32[96,2,8,64]{3,2,1,0:T(8,128)}) fusion(bf16[96,2,8,128]{3,2,1,0:T(8,128)(2,1)S(1)} %bitcast.87, pred[96,64]{1,0:T(8,128)(4,1)} %iota_compare_fusion.5, bf16[96,64,256]{2,1,0:T(8,128)(2,1)} %param.11), kind=kOutput, calls=%fused_computation.59 | convolution fusion | flops 25459200 | bytes 3944448 | tf_op jit(solution)/shard_map/rkgd,rlkd->rkgl/dot_general | solution.py:54
  20.1 0.9 copy.33
  21.2 1.7 fusion.23
  23.0 0.8 copy.36
  23.7 0.8 copy.38
  24.5 2.3 fusion.19
  26.8 0.9 copy.83
  27.7 39.9 %all-gather.2.cloned.1.call-done = bf16[384,2048]{1,0:T(8,128)(2,1)} async-done(((bf16[96,2048]{1,0:T(8,128)(2,1)}), bf16[384,2048]{1,0:T(8,128)(2,1)}) %all-gather.2.cloned.1.call-update) | async-done | bytes 1572880 | tf_op jit(solution)/shard_map/all_gather | solution.py:80
  67.6 6.3 %fusion.44 = f32[384,2048]{1,0:T(8,128)S(1)} fusion(bf16[384,2048]{1,0:T(8,128)(2,1)} %all-gather.2.cloned.1.call-done, bf16[2048,2048]{1,0:T(8,128)(2,1)} %param.17), kind=kOutput, calls=%fused_computation.61 | convolution fusion | flops 3221225472 | bytes 13107200 | tf_op jit(solution)/shard_map/dot_general | solution.py:79
  73.9 73.3 %all_to_all.35 = f32[4,96,2048]{2,1,0:T(8,128)S(1)} all-to-all(f32[4,96,2048]{2,1,0:T(8,128)S(1)} %bitcast.81), channel_id=1, replica_groups=mesh['groups'=2,'batch'=4,'tensor'=4] {'batch'}, dimensions={0} | all-to-all | bytes 6291456 | tf_op jit(solution)/shard_map/all_to_all | solution.py:84
  147.2 1.9 copy.55
  149.1 0.6 copy-done.2
  149.8 0.1 fusion.22
  150.1 0.7 convert_element_type.101
  150.7 3.2 %all-to-all-start.2 = ((bf16[4,1,48]{2,1,0:T(2,128)(2,1)}), bf16[4,1,48]{2,1,0:T(2,128)(2,1)S(1)}, u32[]{:S(2)}, u32[]{:S(2)}) async-start(bf16[4,1,48]{2,1,0:T(2,128)(2,1)} %convert_element_type.101), calls=%async_computation.3 | async-start | bytes 4096 | tf_op jit(solution)/shard_map/all_to_all | solution.py:109
  153.9 1.4 convolution_convert_fusion
  155.3 4.1 %all-to-all-done.2 = bf16[4,1,48]{2,1,0:T(2,128)(2,1)S(1)} async-done(((bf16[4,1,48]{2,1,0:T(2,128)(2,1)}), bf16[4,1,48]{2,1,0:T(2,128)(2,1)S(1)}, u32[]{:S(2)}, u32[]{:S(2)}) %all-to-all-start.2) | async-done | bytes 416 | tf_op jit(solution)/shard_map/all_to_all | solution.py:109
  159.4 4.2 %all-to-all-start.1 = ((bf16[4,48,2048]{2,1,0:T(8,128)(2,1)}), bf16[4,48,2048]{2,1,0:T(8,128)(2,1)}, u32[]{:S(2)}, u32[]{:S(2)}) async-start(bf16[4,48,2048]{2,1,0:T(8,128)(2,1)} %bitcast.82), calls=%async_computation.2 | async-start | bytes 1572864 | tf_op jit(solution)/shard_map/all_to_all | solution.py:108
  163.9 18.3 %all-to-all-done.1 = bf16[4,48,2048]{2,1,0:T(8,128)(2,1)} async-done(((bf16[4,48,2048]{2,1,0:T(8,128)(2,1)}), bf16[4,48,2048]{2,1,0:T(8,128)(2,1)}, u32[]{:S(2)}, u32[]{:S(2)}) %all-to-all-start.1) | async-done | bytes 786464 | tf_op jit(solution)/shard_map/all_to_all | solution.py:108
  182.1 1.9 fusion.45
  184.1 10.7 %psum.7 = bf16[192,64]{0,1:T(8,128)(2,1)S(1)} all-reduce(f32[192,64]{0,1:T(8,128)S(1)} %multiply_reduce_fusion), channel_id=1, replica_groups=mesh['groups'=2,'batch'=4,'tensor'=4] {'tensor'}, use_global_device_ids=true, to_apply=%region_5.6 | all-reduce | flops 12288 | bytes 73728 | tf_op jit(solution)/shard_map/psum | solution.py:19
  194.8 2.2 fusion.32
  197.0 2.6 %fusion = f32[192,1,2048]{2,1,0:T(1,128)S(1)} fusion(bf16[192,4,2048]{2,0,1:T(8,128)(2,1)S(1)} %fusion.32, pred[192,4,1]{1,0,2:T(32,128)(4,1)S(1)} %get-tuple-element.7), kind=kOutput, calls=%fused_computation | convolution fusion | flops 3145728 | bytes 4719360 | tf_op jit(solution)/shard_map/czp,cz->cp/dot_general | solution.py:23
  199.6 0.5 fusion.9
  200.1 23.8 %all_to_all.36 = bf16[4,48,2048]{2,1,0:T(8,128)(2,1)} all-to-all(bf16[4,48,2048]{2,1,0:T(8,128)(2,1)S(1)} %bitcast.84), channel_id=1, replica_groups=mesh['groups'=2,'batch'=4,'tensor'=4] {'batch'}, dimensions={0} | all-to-all | bytes 1572864 | tf_op jit(solution)/shard_map/all_to_all | solution.py:27
  223.9 2.4 %fusion.8 = bf16[96,2048]{1,0:T(8,128)(2,1)} fusion(f32[96,2048]{1,0:T(8,128)} %reduce-scatter.2.cloned.1.call-done, bf16[192,2048]{1,0:T(8,128)(2,1)} %bitcast.83, s32[96]{0:T(128)S(1)} %convert_add_fusion), kind=kOutput, calls=%fused_computation.10 | convolution fusion | flops 75909120 | bytes 1966464 | tf_op jit(solution)/shard_map/dot_general | solution.py:121
  (23 shorter events, 0.8 us)
Async XLA Ops:
  6.5 18.0 %copy-start = (bf16[96,64,256]{2,1,0:T(8,128)(2,1)S(1)}, bf16[96,64,256]{2,1,0:T(8,128)(2,1)}, u32[]{:S(2)}) copy-start(bf16[96,64,256]{2,1,0:T(8,128)(2,1)} %param.12) | copy-start | bytes 9437188
  6.5 61.0 %all-gather.2.cloned.1.call-start = ((), (), s32[]{:S(2)}) async-start(), calls=%async_computation.5 | async-start | bytes 1966080 | tf_op jit(solution)/shard_map/all_gather | solution.py:80
  21.2 2.6 %copy-start.1 = (f32[96,2,8]{2,1,0:T(2,128)}, f32[96,2,8]{2,1,0:T(2,128)S(1)}, u32[]{:S(2)}) copy-start(f32[96,2,8]{2,1,0:T(2,128)S(1)} %copy.34) | copy-start | bytes 18436
  27.6 196.2 %reduce-scatter.2.cloned.1.call-start = ((), (), s32[]{:S(2)}) async-start(), calls=%async_computation.6 | async-start | bytes 3932160 | tf_op jit(solution)/shard_map/reduce_scatter | solution.py:85
  149.1 0.7 copy-start.2
  150.7 8.7 %all-to-all-start.2 = ((bf16[4,1,48]{2,1,0:T(2,128)(2,1)}), bf16[4,1,48]{2,1,0:T(2,128)(2,1)S(1)}, u32[]{:S(2)}, u32[]{:S(2)}) async-start(bf16[4,1,48]{2,1,0:T(2,128)(2,1)} %convert_element_type.101), calls=%async_computation.3 | async-start | bytes 4096 | tf_op jit(solution)/shard_map/all_to_all | solution.py:109
  159.4 22.7 %all-to-all-start.1 = ((bf16[4,48,2048]{2,1,0:T(8,128)(2,1)}), bf16[4,48,2048]{2,1,0:T(8,128)(2,1)}, u32[]{:S(2)}, u32[]{:S(2)}) async-start(bf16[4,48,2048]{2,1,0:T(8,128)(2,1)} %bitcast.82), calls=%async_computation.2 | async-start | bytes 1572864 | tf_op jit(solution)/shard_map/all_to_all | solution.py:108
Sparse Core Ops, SparseCore 0:
  27.8 39.7 all-gather.1
  149.2 37.1 reduce-scatter.1
where the time goes:
time: 234 us; the launch traced here: 233 us
  blocking collectives  108 us (46%)
  waiting for transfers between devices  62.3 us (27%)
  matrix products  26.3 us (11%)
  between operations  13.5 us (6%)
  local copies, waits for them, and re-layouts  11.8 us (5%)
  starting transfers between devices  7.45 us (3%)
  other arithmetic  3.98 us (2%)
    all_to_all x1, blocking collectives, body(): lax.all_to_all(partial_sums, 'batch', split_axis=0, concat_axis=1, tiled=...  73.3 us
    all_gather x1, waiting for transfers between devices, body(): lax.all_gather(attention_output, 'batch', axis=0, tiled=True)  39.9 us
    all_to_all x1, blocking collectives, finish_output(): lax.all_to_all(final_result, 'batch', split_axis=0, concat_axis=0, tiled=...  23.8 us
    all_to_all x1, waiting for transfers between devices, body(): lax.all_to_all(send_rows, 'batch', split_axis=0, concat_axis=0, tiled=True)  18.3 us
    psum x1, blocking collectives, finish_output(): small_product = lax.psum(partial_small, 'tensor').astype(jnp.bfloat16)  10.7 us
    dot_general x1, matrix products, body(): jnp.dot(lax.all_gather(attention_output, 'batch', axis=0, tiled=True), ou...  6.28 us
    dot_general x1, matrix products, body(): jnp.einsum('rkgd,rlkd->rkgl', query_rows, keys, preferred_element_type=jn...  5.22 us
  transfers between devices with their start and end apart: 4, of which 3 were waited for; matrix products, arithmetic and copies ran while one was open for 4% of the time, Pallas kernels for 0%

commit v1 on v0

--- a/solution.py
+++ b/solution.py
@@ -1,6 +1,8 @@
 import jax
 import jax.numpy as jnp
 from jax import lax
+from jax.experimental import pallas as pl
+from jax.experimental.pallas import tpu as pltpu
 from jax.sharding import PartitionSpec as P
 
 HEAD_SIZE = 128
@@ -122,7 +124,416 @@
     return (base_output + adapter_rows).astype(jnp.bfloat16)
 
 
+F32 = jnp.float32
+BF16 = jnp.bfloat16
+PIECES = 3
+STEP_ROWS = 16
+LANES = 128
+
+
+def remote(src, dst, send_sem, recv_sem, batch, tensor):
+    return pltpu.make_async_remote_copy(
+        src_ref=src,
+        dst_ref=dst,
+        send_sem=send_sem,
+        recv_sem=recv_sem,
+        device_id={"batch": batch, "tensor": tensor},
+        device_id_type=pl.DeviceIdType.MESH,
+    )
+
+
+def attend_rows(r0, q_v, k_v, v_v, tk_ref, tv_ref, len_ref, attn_all, z):
+    group = 8
+    rows = group * STEP_ROWS
+    span = 64
+    pos_rows = pl.ds(pl.multiple_of(r0 * span, STEP_ROWS * span), STEP_ROWS * span)
+    req = pl.ds(r0, STEP_ROWS)
+    row = lax.broadcasted_iota(jnp.int32, (rows, LANES), 0)
+    lane = lax.broadcasted_iota(jnp.int32, (rows, LANES), 1)
+    in_step = row % STEP_ROWS
+    pair = in_step // 2
+    lens = jnp.concatenate([len_ref[req, :]] * group, axis=0)
+    valid = ((in_step % 2) == (lane // span)) & ((lane % span) < lens)
+    scale = HEAD_SIZE ** (-0.5)
+    for kv in range(2):
+        cols = slice(kv * HEAD_SIZE, (kv + 1) * HEAD_SIZE)
+        q = jnp.concatenate(
+            [
+                q_v[req, (kv * group + h) * HEAD_SIZE : (kv * group + h + 1) * HEAD_SIZE]
+                for h in range(group)
+            ],
+            axis=0,
+        )
+        s = lax.dot_general(
+            q, k_v[pos_rows, cols], (((1,), (1,)), ((), ())), preferred_element_type=F32
+        )
+        c = s[:, :LANES]
+        for j in range(1, STEP_ROWS // 2):
+            c = jnp.where(pair == j, s[:, j * LANES : (j + 1) * LANES], c)
+        c = jnp.where(valid, c * scale, -jnp.inf)
+        tk = jnp.concatenate([tk_ref[req, cols].astype(F32)] * group, axis=0)
+        own = jnp.sum(q.astype(F32) * tk, axis=1, keepdims=True) * scale
+        top = jnp.maximum(jnp.max(c, axis=1, keepdims=True), own)
+        e = jnp.exp(c - top)
+        own_e = jnp.exp(own - top)
+        total = jnp.sum(e, axis=1, keepdims=True) + own_e
+        p = e / total
+        own_w = (own_e / total).astype(BF16).astype(F32)
+        wide = jnp.concatenate(
+            [jnp.where(pair == j, p, 0.0).astype(BF16) for j in range(STEP_ROWS // 2)], axis=1
+        )
+        o = jnp.dot(wide, v_v[pos_rows, cols], preferred_element_type=F32)
+        tv = jnp.concatenate([tv_ref[req, cols].astype(F32)] * group, axis=0)
+        o = (o + own_w * tv).astype(BF16)
+        for h in range(group):
+            head = kv * group + h
+            attn_all[z, req, head * HEAD_SIZE : (head + 1) * HEAD_SIZE] = o[
+                h * STEP_ROWS : (h + 1) * STEP_ROWS
+            ]
+
+
+def placement(ids, owner, held, rows):
+    low = (owner * held).astype(F32)
+    mine = (ids >= low) & (ids < low + held)
+    tri = (
+        lax.broadcasted_iota(jnp.int32, (rows, rows), 0)
+        > lax.broadcasted_iota(jnp.int32, (rows, rows), 1)
+    )
+    rank = jnp.dot(
+        jnp.where(tri, 1.0, 0.0).astype(BF16),
+        jnp.where(mine, 1.0, 0.0).astype(BF16),
+        preferred_element_type=F32,
+    )
+    slot = lax.broadcasted_iota(jnp.int32, (rows, LANES), 1).astype(F32)
+    return jnp.where(mine & (rank == slot), 1.0, 0.0).astype(BF16)
+
+
+def kernel(
+    q_hbm, k_hbm, v_hbm, tk_ref, tv_ref, len_ref, ids_ref, w_hbm, down_hbm, up_hbm,
+    out_ref,
+    q_v, k_v, v_v, w_v, down_v, up_v,
+    ids_all, attn_all, u_send, u_recv, rs_send, rs_own, rs_recv,
+    lora_send, lora_recv, out_send, out_recv,
+    load_sem, id_ssem, id_rsem, at_ssem, fw_ssem, at_rsem, u_ssem, u_rsem,
+    rs_ssem, rs_rsem, lo_ssem, lo_rsem, out_ssem, out_rsem,
+):
+    z = lax.axis_index("batch")
+    t = lax.axis_index("tensor")
+    rows, width = out_ref.shape
+    n = 4
+    held = down_v.shape[0]
+    rank_width = down_v.shape[2]
+    slots = lora_send.shape[1]
+    quarter = width // n
+    half = rows // 2
+    piece = rows // PIECES
+    span = k_v.shape[0] // rows
+
+    barrier = pltpu.get_barrier_semaphore()
+    for i in range(1, n * n):
+        other = (z * n + t + i) % (n * n)
+        pl.semaphore_signal(
+            barrier,
+            inc=1,
+            device_id={"batch": other // n, "tensor": other % n},
+            device_id_type=pl.DeviceIdType.MESH,
+        )
+
+    loads = [pltpu.make_async_copy(q_hbm, q_v, load_sem.at[0])]
+    for p in range(PIECES):
+        part = pl.ds(p * piece * span, piece * span)
+        loads.append(pltpu.make_async_copy(k_hbm.at[part], k_v.at[part], load_sem.at[1 + 2 * p]))
+        loads.append(pltpu.make_async_copy(v_hbm.at[part], v_v.at[part], load_sem.at[2 + 2 * p]))
+    tail_loads = [
+        pltpu.make_async_copy(down_hbm, down_v, load_sem.at[7]),
+        pltpu.make_async_copy(w_hbm, w_v, load_sem.at[8]),
+        pltpu.make_async_copy(up_hbm, up_v, load_sem.at[9]),
+    ]
+    for load in loads + tail_loads:
+        load.start()
+    ids_all[z] = ids_ref[...]
+
+    def id_copy(i):
+        return remote(ids_all.at[z], ids_all.at[z], id_ssem.at[i - 1], id_rsem.at[z], (z + i) % n, t)
+
+    def own_copy(direction, p):
+        part = attn_all.at[z, pl.ds(p * piece, piece)]
+        to = z + 1 if direction else z - 1
+        return remote(part, part, at_ssem.at[direction, p], at_rsem.at[z, p], to, t)
+
+    loads[0].wait()
+    for p in range(PIECES):
+        loads[1 + 2 * p].wait()
+        loads[2 + 2 * p].wait()
+
+        def step(i, carry):
+            r0 = pl.multiple_of(i * STEP_ROWS, STEP_ROWS)
+            attend_rows(r0, q_v, k_v, v_v, tk_ref, tv_ref, len_ref, attn_all, z)
+            return carry
+
+        per = piece // STEP_ROWS
+        lax.fori_loop(p * per, (p + 1) * per, step, 0)
+        if p == 0:
+            pl.semaphore_wait(barrier, n * n - 1)
+            for i in range(1, n):
+                id_copy(i).start()
+
+        @pl.when(z < n - 1)
+        def _():
+            own_copy(1, p).start()
+
+        @pl.when(z > 0)
+        def _():
+            own_copy(0, p).start()
+
+    blocks = [z, z + 1 - 2 * (z % 2), 2 - z // 2, 3 - 3 * (z // 2)]
+
+    def block_ids(b):
+        return ids_all[b].astype(F32)
+
+    def adapter_mask(ids, j):
+        return ids[:, :rank_width] == (z * held + j).astype(F32)
+
+    def forward(k, p, to):
+        b = blocks[k]
+        part = attn_all.at[b, pl.ds(p * piece, piece)]
+        return remote(part, part, fw_ssem.at[k, p], at_rsem.at[b, p], to, t)
+
+    def u_copy(k, i):
+        return remote(
+            u_send.at[k], u_recv.at[k, t], u_ssem.at[k, i - 1], u_rsem.at[k, t], z, (t + i) % n
+        )
+
+    def rs_copy(k, i):
+        return remote(
+            rs_send.at[k, i - 1], rs_recv.at[k, t], rs_ssem.at[k, i - 1], rs_rsem.at[k, t],
+            z, (t + i) % n,
+        )
+
+    def lora_copy(k):
+        return remote(
+            lora_send.at[k], lora_recv.at[z], lo_ssem.at[k], lo_rsem.at[z], blocks[k], t
+        )
+
+    def out_copy(k):
+        return remote(out_send.at[k], out_recv.at[t], out_ssem.at[k], out_rsem.at[t], blocks[k], z)
+
+    middle = (z * (n - 1 - z)) > 0
+
+    def relay_to(k):
+        return z - 1 + 2 * (z % 2) if k == 1 else z - 1 + 2 * (z // 2)
+
+    def main(k):
+        b = blocks[k]
+        if k > 0:
+            for p in range(PIECES):
+                forward(k, p, z).wait_recv()
+
+                @pl.when(middle)
+                def _():
+                    forward(k, p, relay_to(k)).start()
+
+            remote(ids_all.at[b], ids_all.at[b], id_ssem.at[0], id_rsem.at[b], z, t).wait_recv()
+        x = attn_all[b]
+        ids = block_ids(b)
+        u = jnp.zeros((rows, rank_width), F32)
+        for j in range(held):
+            uj = jnp.dot(x, down_v[j], preferred_element_type=F32)
+            u = jnp.where(adapter_mask(ids, j), uj, u)
+        u_send[k] = jnp.concatenate([u[:half], u[half:]], axis=1)
+        for i in range(1, n):
+            u_copy(k, i).start()
+
+        def project(i, carry):
+            q = (t + i) % n
+            cols = pl.ds(pl.multiple_of(q * quarter, quarter), quarter)
+            part = jnp.dot(attn_all[b], w_v[:, cols], preferred_element_type=F32)
+            rs_send[k, i - 1] = part.astype(BF16)
+            rs_copy(k, i).start()
+            return carry
+
+        lax.fori_loop(1, n, project, 0)
+        cols = pl.ds(pl.multiple_of(t * quarter, quarter), quarter)
+        rs_own[k] = jnp.dot(attn_all[b], w_v[:, cols], preferred_element_type=F32)
+
+    def post(k):
+        b = blocks[k]
+        total = u_send[k]
+        for i in range(1, n):
+            src = (t + i) % n
+            remote(
+                u_recv.at[k, src], u_recv.at[k, src], u_ssem.at[k, i - 1], u_rsem.at[k, src], z, src
+            ).wait_recv()
+            total = total + u_recv[k, src]
+        u = jnp.concatenate([total[:, :rank_width], total[:, rank_width:]], axis=0)
+        ids = block_ids(b)
+        place = placement(ids, z, held, rows)
+        compact = []
+        for j in range(held):
+            uj = jnp.where(adapter_mask(ids, j), u, 0.0).astype(BF16)
+            cj = lax.dot_general(place, uj, (((0,), (0,)), ((), ())), preferred_element_type=F32)
+            compact.append(cj[:slots].astype(BF16))
+        target = lora_recv.at[z] if k == 0 else lora_send.at[k]
+        for q in range(n):
+            cs = slice(q * quarter, (q + 1) * quarter)
+            acc = jnp.dot(compact[0], up_v[0, :, cs], preferred_element_type=F32)
+            for j in range(1, held):
+                acc = acc + jnp.dot(compact[j], up_v[j, :, cs], preferred_element_type=F32)
+            target[:, cs] = (adapter_scale * acc).astype(BF16)
+        if k > 0:
+            lora_copy(k).start()
+
+        sums = rs_own[k]
+        for i in range(1, n):
+            src = (t + i) % n
+            remote(
+                rs_recv.at[k, src], rs_recv.at[k, src], rs_ssem.at[k, i - 1], rs_rsem.at[k, src],
+                z, src,
+            ).wait_recv()
+            sums = sums + rs_recv[k, src].astype(F32)
+        out_send[k] = sums.astype(BF16)
+        if k > 0:
+            out_copy(k).start()
+        else:
+
+            @pl.when(t != z)
+            def _():
+                out_copy(0).start()
+
+            @pl.when(t == z)
+            def _():
+                out_recv[t] = out_send[0]
+
+    for load in tail_loads:
+        load.wait()
+    main(0)
+    for k in range(1, n):
+        main(k)
+        post(k - 1)
+    post(n - 1)
+
+    ids = block_ids(z)
+    places = [placement(ids, z * 0 + o, held, rows)[:, :slots] for o in range(n)]
+    for k in range(1, n):
+        b = blocks[k]
+        remote(
+            lora_recv.at[b], lora_recv.at[b], lo_ssem.at[k], lo_rsem.at[b], z, t
+        ).wait_recv()
+    for src in range(n):
+
+        def arrive(src=src):
+            remote(
+                out_recv.at[src], out_recv.at[src], out_ssem.at[0], out_rsem.at[src], z, t
+            ).wait_recv()
+
+        pl.when((z - t) * (z - t) + (src - t) * (src - t) > 0)(arrive)
+        cs = slice(src * quarter, (src + 1) * quarter)
+        acc = out_recv[src].astype(F32)
+        for o in range(n):
+            acc = acc + jnp.dot(places[o], lora_recv[o, :, cs], preferred_element_type=F32)
+        out_ref[:, cs] = acc.astype(BF16)
+
+    for i in range(1, n):
+        id_copy(i).wait_send()
+    for p in range(PIECES):
+
+        @pl.when(z < n - 1)
+        def _():
+            own_copy(1, p).wait_send()
+
+        @pl.when(z > 0)
+        def _():
+            own_copy(0, p).wait_send()
+
+        @pl.when(middle)
+        def _():
+            for k in range(1, n):
+                forward(k, p, relay_to(k)).wait_send()
+
+    for k in range(n):
+        for i in range(1, n):
+            u_copy(k, i).wait_send()
+            rs_copy(k, i).wait_send()
+        if k > 0:
+            lora_copy(k).wait_send()
+            out_copy(k).wait_send()
+        else:
+
+            @pl.when(t != z)
+            def _():
+                out_copy(0).wait_send()
+
+
+def fused_body(
+    queries, cached_keys, cached_values, token_key, token_value, lengths, adapter_index,
+    output_weight, adapter_down, adapter_up,
+):
+    rows, width = queries.shape
+    span, kv_width = cached_keys.shape[1:]
+    n = lax.axis_size("batch")
+    held, _, rank_width = adapter_down.shape
+    slots = max(2, 2 * rows // n)
+    quarter = width // n
+    lens = jnp.broadcast_to(lengths[:, None], (rows, LANES))
+    ids = jnp.broadcast_to(adapter_index[:, None], (rows, LANES)).astype(BF16)
+    vmem = pl.BlockSpec(memory_space=pltpu.VMEM)
+    hbm = pl.BlockSpec(memory_space=pl.ANY)
+    dma = pltpu.SemaphoreType.DMA
+    flops = 2 * rows * n * width * (width + held * rank_width)
+    return pl.pallas_call(
+        kernel,
+        out_shape=jax.ShapeDtypeStruct((rows, width), BF16),
+        in_specs=[hbm, hbm, hbm, vmem, vmem, vmem, vmem, hbm, hbm, hbm],
+        out_specs=vmem,
+        scratch_shapes=[
+            pltpu.VMEM((rows, width), BF16),
+            pltpu.VMEM((rows * span, kv_width), BF16),
+            pltpu.VMEM((rows * span, kv_width), BF16),
+            pltpu.VMEM(output_weight.shape, BF16),
+            pltpu.VMEM(adapter_down.shape, BF16),
+            pltpu.VMEM(adapter_up.shape, BF16),
+            pltpu.VMEM((n, rows, LANES), BF16),
+            pltpu.VMEM((n, rows, width), BF16),
+            pltpu.VMEM((n, rows // 2, 2 * rank_width), F32),
+            pltpu.VMEM((n, n, rows // 2, 2 * rank_width), F32),
+            pltpu.VMEM((n, n - 1, rows, quarter), BF16),
+            pltpu.VMEM((n, rows, quarter), F32),
+            pltpu.VMEM((n, n, rows, quarter), BF16),
+            pltpu.VMEM((n, slots, width), BF16),
+            pltpu.VMEM((n, slots, width), BF16),
+            pltpu.VMEM((n, rows, quarter), BF16),
+            pltpu.VMEM((n, rows, quarter), BF16),
+            dma((10,)),
+            dma((n - 1,)), dma((n,)),
+            dma((2, PIECES)), dma((n, PIECES)), dma((n, PIECES)),
+            dma((n, n - 1)), dma((n, n)),
+            dma((n, n - 1)), dma((n, n)),
+            dma((n,)), dma((n,)),
+            dma((n,)), dma((n,)),
+        ],
+        cost_estimate=pl.CostEstimate(
+            flops=flops, bytes_accessed=2 * (width * width + 2 * rows * span * kv_width),
+            transcendentals=0,
+        ),
+        compiler_params=pltpu.CompilerParams(
+            collective_id=0, has_side_effects=True, vmem_limit_bytes=50 * 2**20
+        ),
+    )(
+        queries,
+        cached_keys.reshape(rows * span, kv_width),
+        cached_values.reshape(rows * span, kv_width),
+        token_key,
+        token_value,
+        lens,
+        ids,
+        output_weight,
+        adapter_down,
+        adapter_up,
+    )
+
+
 def solution(mesh):
+    fused = mesh.shape["batch"] == 4 and mesh.shape["tensor"] == 4
     placed = (
         P(("groups", "batch"), "tensor"),
         P(("groups", "batch"), None, "tensor"),
@@ -136,7 +547,7 @@
         P("batch", None, "tensor"),
     )
     return jax.shard_map(
-        body,
+        fused_body if fused else body,
         mesh=mesh,
         in_specs=placed,
         out_specs=P(("groups", "batch"), "tensor"),

time: 234 us -> 80.1 us (0.34)
  blocking collectives: 108 us -> 0 us
  Pallas kernels: 0 us -> 71 us
  waiting for transfers between devices: 62.3 us -> 0 us
  matrix products: 26.3 us -> 0 us
  between operations: 13.5 us -> 0.05 us
  starting transfers between devices: 7.45 us -> 0 us
  local copies, waits for them, and re-layouts: 11.8 us -> 7.94 us
  other arithmetic: 3.98 us -> 0.77 us
    all_to_all x2 -> x0, blocking collectives: 97.1 us -> none  [the longest x1 73.3 us: body(): lax.all_to_all(partial_sums, 'batch', split_axis=0, concat_axis=1, tiled=...]
    pallas_call x0 -> x1, Pallas kernels: none -> 71 us  [fused_body(): pl.pallas_call(kernel, out_shape=jax.ShapeDtypeStruct((rows, width), BF16...]
    all_gather x1 -> x0, waiting for transfers between devices: 39.9 us -> none  [body(): lax.all_gather(attention_output, 'batch', axis=0, tiled=True)]
    dot_general x9 -> x0, matrix products: 24.3 us -> none  [the longest x1 6.28 us: body(): jnp.dot(lax.all_gather(attention_output, 'batch', axis=0, tiled=True), ou...]
    all_to_all x2 -> x0, waiting for transfers between devices: 22.3 us -> none  [the longest x1 18.3 us: body(): lax.all_to_all(send_rows, 'batch', split_axis=0, concat_axis=0, tiled=True)]
    psum x1 -> x0, blocking collectives: 10.7 us -> none  [finish_output(): small_product = lax.psum(partial_small, 'tensor').astype(jnp.bfloat16)]
    all_to_all x2 -> x0, starting transfers between devices: 7.41 us -> none  [the longest x1 4.19 us: body(): lax.all_to_all(send_rows, 'batch', split_axis=0, concat_axis=0, tiled=True)]
    unnamed x9 -> x14, local copies, waits for them, and re-layouts: 2.63 us -> 5.9 us
  transfers between devices with their start and end apart: 4 -> 0, of which waited for: 3 -> 0; matrix products, arithmetic and copies ran while one was open for 4% -> 0% of each run, Pallas kernels for 0% -> 0%
where the time goes in v1:
time: 80.1 us; the launch traced here: 79.7 us
  Pallas kernels  71 us (89%)
  local copies, waits for them, and re-layouts  7.94 us (10%)
    pallas_call x1, Pallas kernels, fused_body(): pl.pallas_call(kernel, out_shape=jax.ShapeDtypeStruct((rows, width), BF16...  71 us
    unnamed x14, local copies, waits for them, and re-layouts  5.9 us

profile of v1, /device:TPU:0, one launch (start us, length us, event | category | flops | bytes accessed | tf_op | source)
XLA Modules:
  0.0 79.7 jit_solution(7169903237753843148)
XLA Ops:
  0.0 0.0 copy-start
  0.0 0.0 copy-start.1
  0.0 0.8 convert_element_type.3
  0.8 0.7 broadcast_in_dim.5.ids_ref
  1.5 1.4 %broadcast_in_dim.4.len_ref = s32[96,128]{1,0:T(8,128)} broadcast(s32[96]{0:T(128)} %param.15), dimensions={0} | broadcast | bytes 49536 | tf_op jit(solution)/shard_map/broadcast_in_dim | solution.py:477
  2.8 2.0 %copy.11.down_hbm = bf16[4,2048,64]{2,1,0:T(8,128)(2,1)S(1)} copy(bf16[4,2048,64]{1,2,0:T(8,128)(2,1)} %param.18) | data formatting | bytes 2097152 | tf_op args[8]
  4.8 0.0 copy-done
  4.9 0.0 copy-done.1
  4.9 0.0 copy-start.2
  4.9 0.8 copy-done.2
  5.7 0.0 copy-start.3
  5.7 0.7 copy-done.3
  6.4 0.0 copy-start.4
  6.4 0.8 copy-done.4
  7.2 0.0 copy-start.5
  7.2 0.8 copy-done.5
  8.0 71.0 %shard_map.100 = bf16[96,2048]{1,0:T(8,128)(2,1)S(1)} custom-call(bf16[96,2048]{1,0:T(8,128)(2,1)S(1)} %copy-done.1, bf16[6144,256]{1,0:T(8,128)(2,1)} %bitcast.2, bf16[6144,256]{1,0:T(8,128)(2,1)} %bitcast.3, bf16[96,256]{1,0:T(8,128)(2,1)S(1)} %copy-done.4, bf16[96,256]{1,0:T(8,128)(2,1)S(1)} %copy-done.5, s32[96,128]{1,0:T(8,128)S(1)} %copy-done.2, ...), custom_call_target="tpu_custom_call" | custom-call | flops 3623878656 | bytes 14680064 | tf_op jit(solution)/shard_map/pallas_call | solution.py:483
  79.0 0.7 copy.13
Async XLA Ops:
  0.0 4.8 %copy-start = (bf16[4,64,2048]{2,1,0:T(8,128)(2,1)S(1)}, bf16[4,64,2048]{2,1,0:T(8,128)(2,1)}, u32[]{:S(2)}) copy-start(bf16[4,64,2048]{2,1,0:T(8,128)(2,1)} %up_hbm.1) | copy-start | bytes 3145732
  0.0 4.9 %copy-start.1 = (bf16[96,2048]{1,0:T(8,128)(2,1)S(1)}, bf16[96,2048]{1,0:T(8,128)(2,1)}, u32[]{:S(2)}) copy-start(bf16[96,2048]{1,0:T(8,128)(2,1)} %q_hbm.1) | copy-start | bytes 1179652
  4.9 0.8 %copy-start.2 = (s32[96,128]{1,0:T(8,128)S(1)}, s32[96,128]{1,0:T(8,128)}, u32[]{:S(2)}) copy-start(s32[96,128]{1,0:T(8,128)} %broadcast_in_dim.4.len_ref) | copy-start | bytes 147460
  5.7 0.7 copy-start.3
  6.4 0.8 %copy-start.4 = (bf16[96,256]{1,0:T(8,128)(2,1)S(1)}, bf16[96,256]{1,0:T(8,128)(2,1)}, u32[]{:S(2)}) copy-start(bf16[96,256]{1,0:T(8,128)(2,1)} %tk_ref.1) | copy-start | bytes 147460
  7.2 0.8 %copy-start.5 = (bf16[96,256]{1,0:T(8,128)(2,1)S(1)}, bf16[96,256]{1,0:T(8,128)(2,1)}, u32[]{:S(2)}) copy-start(bf16[96,256]{1,0:T(8,128)(2,1)} %tv_ref.1) | copy-start | bytes 147460

commit v2 on v1

--- a/solution.py
+++ b/solution.py
@@ -153,7 +153,7 @@
     in_step = row % STEP_ROWS
     pair = in_step // 2
     lens = jnp.concatenate([len_ref[req, :]] * group, axis=0)
-    valid = ((in_step % 2) == (lane // span)) & ((lane % span) < lens)
+    valid = ((in_step % 2) == (lane // span)) & ((lane % span).astype(F32) < lens)
     scale = HEAD_SIZE ** (-0.5)
     for kv in range(2):
         cols = slice(kv * HEAD_SIZE, (kv + 1) * HEAD_SIZE)
@@ -209,9 +209,9 @@
 
 
 def kernel(
-    q_hbm, k_hbm, v_hbm, tk_ref, tv_ref, len_ref, ids_ref, w_hbm, down_hbm, up_hbm,
+    q_hbm, k_hbm, v_hbm, tk_hbm, tv_hbm, len_hbm, ids_hbm, w_hbm, down_hbm, up_hbm,
     out_ref,
-    q_v, k_v, v_v, w_v, down_v, up_v,
+    q_v, k_v, v_v, w_v, down_v, up_v, tk_ref, tv_ref, len_v, ids_v, len_ref,
     ids_all, attn_all, u_send, u_recv, rs_send, rs_own, rs_recv,
     lora_send, lora_recv, out_send, out_recv,
     load_sem, id_ssem, id_rsem, at_ssem, fw_ssem, at_rsem, u_ssem, u_rsem,
@@ -222,7 +222,7 @@
     rows, width = out_ref.shape
     n = 4
     held = down_v.shape[0]
-    rank_width = down_v.shape[2]
+    rank_width = down_v.shape[1]
     slots = lora_send.shape[1]
     quarter = width // n
     half = rows // 2
@@ -239,6 +239,12 @@
             device_id_type=pl.DeviceIdType.MESH,
         )
 
+    small_loads = [
+        pltpu.make_async_copy(len_hbm, len_v, load_sem.at[10]),
+        pltpu.make_async_copy(ids_hbm, ids_v, load_sem.at[11]),
+        pltpu.make_async_copy(tk_hbm, tk_ref, load_sem.at[12]),
+        pltpu.make_async_copy(tv_hbm, tv_ref, load_sem.at[13]),
+    ]
     loads = [pltpu.make_async_copy(q_hbm, q_v, load_sem.at[0])]
     for p in range(PIECES):
         part = pl.ds(p * piece * span, piece * span)
@@ -249,9 +255,16 @@
         pltpu.make_async_copy(w_hbm, w_v, load_sem.at[8]),
         pltpu.make_async_copy(up_hbm, up_v, load_sem.at[9]),
     ]
-    for load in loads + tail_loads:
+    for load in small_loads + loads:
         load.start()
-    ids_all[z] = ids_ref[...]
+    for load in small_loads:
+        load.wait()
+
+    def by_row(line):
+        return jnp.transpose(jnp.broadcast_to(line.astype(F32), (LANES, rows)))
+
+    len_ref[...] = by_row(len_v[...])
+    ids_all[z] = by_row(ids_v[...]).astype(BF16)
 
     def id_copy(i):
         return remote(ids_all.at[z], ids_all.at[z], id_ssem.at[i - 1], id_rsem.at[z], (z + i) % n, t)
@@ -265,6 +278,9 @@
     for p in range(PIECES):
         loads[1 + 2 * p].wait()
         loads[2 + 2 * p].wait()
+        if p == 0:
+            for load in tail_loads:
+                load.start()
 
         def step(i, carry):
             r0 = pl.multiple_of(i * STEP_ROWS, STEP_ROWS)
@@ -323,22 +339,29 @@
     def relay_to(k):
         return z - 1 + 2 * (z % 2) if k == 1 else z - 1 + 2 * (z // 2)
 
+    def relay(k, pieces):
+        @pl.when(middle)
+        def _():
+            for p in pieces:
+                forward(k, p, z).wait_recv()
+                forward(k, p, relay_to(k)).start()
+
     def main(k):
         b = blocks[k]
         if k > 0:
-            for p in range(PIECES):
-                forward(k, p, z).wait_recv()
-
-                @pl.when(middle)
-                def _():
-                    forward(k, p, relay_to(k)).start()
+            @pl.when(jnp.logical_not(middle))
+            def _():
+                for p in range(PIECES):
+                    forward(k, p, z).wait_recv()
 
             remote(ids_all.at[b], ids_all.at[b], id_ssem.at[0], id_rsem.at[b], z, t).wait_recv()
         x = attn_all[b]
         ids = block_ids(b)
         u = jnp.zeros((rows, rank_width), F32)
         for j in range(held):
-            uj = jnp.dot(x, down_v[j], preferred_element_type=F32)
+            uj = lax.dot_general(
+                x, down_v[j], (((1,), (1,)), ((), ())), preferred_element_type=F32
+            )
             u = jnp.where(adapter_mask(ids, j), uj, u)
         u_send[k] = jnp.concatenate([u[:half], u[half:]], axis=1)
         for i in range(1, n):
@@ -407,10 +430,18 @@
     for load in tail_loads:
         load.wait()
     main(0)
-    for k in range(1, n):
-        main(k)
-        post(k - 1)
-    post(n - 1)
+    for p in range(PIECES):
+        relay(1, [p])
+        relay(2, [p])
+    main(1)
+    relay(3, [0])
+    post(0)
+    relay(3, range(1, PIECES))
+    main(2)
+    post(1)
+    main(3)
+    post(2)
+    post(3)
 
     ids = block_ids(z)
     places = [placement(ids, z * 0 + o, held, rows)[:, :slots] for o in range(n)]
@@ -474,8 +505,6 @@
     held, _, rank_width = adapter_down.shape
     slots = max(2, 2 * rows // n)
     quarter = width // n
-    lens = jnp.broadcast_to(lengths[:, None], (rows, LANES))
-    ids = jnp.broadcast_to(adapter_index[:, None], (rows, LANES)).astype(BF16)
     vmem = pl.BlockSpec(memory_space=pltpu.VMEM)
     hbm = pl.BlockSpec(memory_space=pl.ANY)
     dma = pltpu.SemaphoreType.DMA
@@ -483,15 +512,20 @@
     return pl.pallas_call(
         kernel,
         out_shape=jax.ShapeDtypeStruct((rows, width), BF16),
-        in_specs=[hbm, hbm, hbm, vmem, vmem, vmem, vmem, hbm, hbm, hbm],
+        in_specs=[hbm] * 10,
         out_specs=vmem,
         scratch_shapes=[
             pltpu.VMEM((rows, width), BF16),
             pltpu.VMEM((rows * span, kv_width), BF16),
             pltpu.VMEM((rows * span, kv_width), BF16),
             pltpu.VMEM(output_weight.shape, BF16),
-            pltpu.VMEM(adapter_down.shape, BF16),
+            pltpu.VMEM((held, rank_width, width), BF16),
             pltpu.VMEM(adapter_up.shape, BF16),
+            pltpu.VMEM(token_key.shape, BF16),
+            pltpu.VMEM(token_value.shape, BF16),
+            pltpu.VMEM((1, rows), jnp.int32),
+            pltpu.VMEM((1, rows), jnp.int32),
+            pltpu.VMEM((rows, LANES), F32),
             pltpu.VMEM((n, rows, LANES), BF16),
             pltpu.VMEM((n, rows, width), BF16),
             pltpu.VMEM((n, rows // 2, 2 * rank_width), F32),
@@ -503,7 +537,7 @@
             pltpu.VMEM((n, slots, width), BF16),
             pltpu.VMEM((n, rows, quarter), BF16),
             pltpu.VMEM((n, rows, quarter), BF16),
-            dma((10,)),
+            dma((14,)),
             dma((n - 1,)), dma((n,)),
             dma((2, PIECES)), dma((n, PIECES)), dma((n, PIECES)),
             dma((n, n - 1)), dma((n, n)),
@@ -516,7 +550,7 @@
             transcendentals=0,
         ),
         compiler_params=pltpu.CompilerParams(
-            collective_id=0, has_side_effects=True, vmem_limit_bytes=50 * 2**20
+            collective_id=0, has_side_effects=True, vmem_limit_bytes=62 * 2**20
         ),
     )(
         queries,
@@ -524,10 +558,10 @@
         cached_values.reshape(rows * span, kv_width),
         token_key,
         token_value,
-        lens,
-        ids,
+        lengths.reshape(1, rows),
+        adapter_index.reshape(1, rows),
         output_weight,
-        adapter_down,
+        adapter_down.transpose(0, 2, 1),
         adapter_up,
     )
 

time: 80.1 us -> 63.6 us (0.79)
  Pallas kernels: 71 us -> 61.7 us
  local copies, waits for them, and re-layouts: 7.94 us -> 1.77 us
    pallas_call x1, Pallas kernels: 71 us -> 61.7 us  [fused_body(): pl.pallas_call(kernel, out_shape=jax.ShapeDtypeStruct((rows, width), BF16...]
    unnamed x14 -> x1, local copies, waits for them, and re-layouts: 5.9 us -> 1.77 us
    broadcast_in_dim x2 -> x0, local copies, waits for them, and re-layouts: 2.04 us -> none  [the longest x1 1.35 us: fused_body(): lens = jnp.broadcast_to(lengths[:, None], (rows, LANES))]
where the time goes in v2:
time: 63.6 us; the launch traced here: 63.5 us
  Pallas kernels  61.7 us (97%)
  local copies, waits for them, and re-layouts  1.77 us (3%)
    pallas_call x1, Pallas kernels, fused_body(): pl.pallas_call(kernel, out_shape=jax.ShapeDtypeStruct((rows, width), BF16...  61.7 us
    unnamed x1, local copies, waits for them, and re-layouts  1.77 us

profile of v2, /device:TPU:0, one launch (start us, length us, event | category | flops | bytes accessed | tf_op | source)
XLA Modules:
  0.0 63.5 jit_solution(2399892781574181449)
XLA Ops:
  0.0 61.7 %shard_map.100 = bf16[96,2048]{1,0:T(8,128)(2,1)} custom-call(bf16[96,2048]{1,0:T(8,128)(2,1)} %q_hbm.1, bf16[6144,256]{1,0:T(8,128)(2,1)} %bitcast.5, bf16[6144,256]{1,0:T(8,128)(2,1)} %bitcast.6, bf16[96,256]{1,0:T(8,128)(2,1)} %tk_hbm.1, bf16[96,256]{1,0:T(8,128)(2,1)} %tv_hbm.1, s32[1,96]{1,0:T(1,128)} %bitcast.8, s32[1,96]{1,0:T(1,128)} %bitcast.9, ...), custom_call_target="tpu_custom_call" | custom-call | flops 3623878656 | bytes 14680064 | tf_op jit(solution)/shard_map/pallas_call | solution.py:512
  61.7 1.8 %copy.12 = bf16[96,2048]{1,0:T(8,128)(2,1)} copy(bf16[96,2048]{1,0:T(8,128)(2,1)} %shard_map.100) | data formatting | bytes 786432

commit v3 on v2

--- a/solution.py
+++ b/solution.py
@@ -126,7 +126,7 @@
 
 F32 = jnp.float32
 BF16 = jnp.bfloat16
-PIECES = 3
+PIECES = 6
 STEP_ROWS = 16
 LANES = 128
 
@@ -192,7 +192,7 @@
             ]
 
 
-def placement(ids, owner, held, rows):
+def owner_ranks(ids, owner, held, rows):
     low = (owner * held).astype(F32)
     mine = (ids >= low) & (ids < low + held)
     tri = (
@@ -204,8 +204,7 @@
         jnp.where(mine, 1.0, 0.0).astype(BF16),
         preferred_element_type=F32,
     )
-    slot = lax.broadcasted_iota(jnp.int32, (rows, LANES), 1).astype(F32)
-    return jnp.where(mine & (rank == slot), 1.0, 0.0).astype(BF16)
+    return mine, rank
 
 
 def kernel(
@@ -213,7 +212,7 @@
     out_ref,
     q_v, k_v, v_v, w_v, down_v, up_v, tk_ref, tv_ref, len_v, ids_v, len_ref,
     ids_all, attn_all, u_send, u_recv, rs_send, rs_own, rs_recv,
-    lora_send, lora_recv, out_send, out_recv,
+    lora_send, lora_recv, out_send, out_recv, place_v, own_place, lora_sum,
     load_sem, id_ssem, id_rsem, at_ssem, fw_ssem, at_rsem, u_ssem, u_rsem,
     rs_ssem, rs_rsem, lo_ssem, lo_rsem, out_ssem, out_rsem,
 ):
@@ -221,8 +220,8 @@
     t = lax.axis_index("tensor")
     rows, width = out_ref.shape
     n = 4
-    held = down_v.shape[0]
-    rank_width = down_v.shape[1]
+    held = 4
+    rank_width = down_v.shape[0] // held
     slots = lora_send.shape[1]
     quarter = width // n
     half = rows // 2
@@ -240,10 +239,10 @@
         )
 
     small_loads = [
-        pltpu.make_async_copy(len_hbm, len_v, load_sem.at[10]),
-        pltpu.make_async_copy(ids_hbm, ids_v, load_sem.at[11]),
-        pltpu.make_async_copy(tk_hbm, tk_ref, load_sem.at[12]),
-        pltpu.make_async_copy(tv_hbm, tv_ref, load_sem.at[13]),
+        pltpu.make_async_copy(len_hbm, len_v, load_sem.at[13]),
+        pltpu.make_async_copy(ids_hbm, ids_v, load_sem.at[14]),
+        pltpu.make_async_copy(tk_hbm, tk_ref, load_sem.at[15]),
+        pltpu.make_async_copy(tv_hbm, tv_ref, load_sem.at[16]),
     ]
     loads = [pltpu.make_async_copy(q_hbm, q_v, load_sem.at[0])]
     for p in range(PIECES):
@@ -251,9 +250,9 @@
         loads.append(pltpu.make_async_copy(k_hbm.at[part], k_v.at[part], load_sem.at[1 + 2 * p]))
         loads.append(pltpu.make_async_copy(v_hbm.at[part], v_v.at[part], load_sem.at[2 + 2 * p]))
     tail_loads = [
-        pltpu.make_async_copy(down_hbm, down_v, load_sem.at[7]),
-        pltpu.make_async_copy(w_hbm, w_v, load_sem.at[8]),
-        pltpu.make_async_copy(up_hbm, up_v, load_sem.at[9]),
+        pltpu.make_async_copy(down_hbm, down_v, load_sem.at[17]),
+        pltpu.make_async_copy(w_hbm, w_v, load_sem.at[18]),
+        pltpu.make_async_copy(up_hbm, up_v, load_sem.at[19]),
     ]
     for load in small_loads + loads:
         load.start()
@@ -307,8 +306,13 @@
     def block_ids(b):
         return ids_all[b].astype(F32)
 
-    def adapter_mask(ids, j):
-        return ids[:, :rank_width] == (z * held + j).astype(F32)
+    def adapter_mask(ids):
+        wide = jnp.concatenate([ids, ids], axis=1)
+        lane = lax.broadcasted_iota(jnp.int32, wide.shape, 1)
+        return wide == (z * held + lane // rank_width).astype(F32)
+
+    def slot_rows(owner):
+        return pl.ds(pl.multiple_of(owner * slots, slots), slots)
 
     def forward(k, p, to):
         b = blocks[k]
@@ -328,7 +332,7 @@
 
     def lora_copy(k):
         return remote(
-            lora_send.at[k], lora_recv.at[z], lo_ssem.at[k], lo_rsem.at[z], blocks[k], t
+            lora_send.at[k], lora_recv.at[slot_rows(z)], lo_ssem.at[k], lo_rsem.at[z], blocks[k], t
         )
 
     def out_copy(k):
@@ -354,15 +358,14 @@
                 for p in range(PIECES):
                     forward(k, p, z).wait_recv()
 
-            remote(ids_all.at[b], ids_all.at[b], id_ssem.at[0], id_rsem.at[b], z, t).wait_recv()
         x = attn_all[b]
         ids = block_ids(b)
-        u = jnp.zeros((rows, rank_width), F32)
-        for j in range(held):
-            uj = lax.dot_general(
-                x, down_v[j], (((1,), (1,)), ((), ())), preferred_element_type=F32
-            )
-            u = jnp.where(adapter_mask(ids, j), uj, u)
+        u = lax.dot_general(
+            x, down_v[...], (((1,), (1,)), ((), ())), preferred_element_type=F32
+        )
+        u = jnp.where(adapter_mask(ids), u, 0.0)
+        u = u[:, :LANES] + u[:, LANES:]
+        u = u[:, :rank_width] + u[:, rank_width:]
         u_send[k] = jnp.concatenate([u[:half], u[half:]], axis=1)
         for i in range(1, n):
             u_copy(k, i).start()
@@ -389,19 +392,16 @@
             ).wait_recv()
             total = total + u_recv[k, src]
         u = jnp.concatenate([total[:, :rank_width], total[:, rank_width:]], axis=0)
-        ids = block_ids(b)
-        place = placement(ids, z, held, rows)
-        compact = []
-        for j in range(held):
-            uj = jnp.where(adapter_mask(ids, j), u, 0.0).astype(BF16)
-            cj = lax.dot_general(place, uj, (((0,), (0,)), ((), ())), preferred_element_type=F32)
-            compact.append(cj[:slots].astype(BF16))
-        target = lora_recv.at[z] if k == 0 else lora_send.at[k]
+        u = jnp.concatenate([u, u], axis=1)
+        u = jnp.concatenate([u, u], axis=1)
+        u = jnp.where(adapter_mask(block_ids(b)), u, 0.0).astype(BF16)
+        compact = lax.dot_general(
+            place_v[k], u, (((0,), (0,)), ((), ())), preferred_element_type=F32
+        )[:slots].astype(BF16)
+        target = lora_recv.at[slot_rows(z)] if k == 0 else lora_send.at[k]
         for q in range(n):
             cs = slice(q * quarter, (q + 1) * quarter)
-            acc = jnp.dot(compact[0], up_v[0, :, cs], preferred_element_type=F32)
-            for j in range(1, held):
-                acc = acc + jnp.dot(compact[j], up_v[j, :, cs], preferred_element_type=F32)
+            acc = jnp.dot(compact, up_v[:, cs], preferred_element_type=F32)
             target[:, cs] = (adapter_scale * acc).astype(BF16)
         if k > 0:
             lora_copy(k).start()
@@ -430,26 +430,42 @@
     for load in tail_loads:
         load.wait()
     main(0)
+    for k in range(1, n):
+        b = blocks[k]
+        remote(ids_all.at[b], ids_all.at[b], id_ssem.at[0], id_rsem.at[b], z, t).wait_recv()
+    slot = lax.broadcasted_iota(jnp.int32, (rows, LANES), 1).astype(F32)
+    for k in range(n):
+        mine, rank = owner_ranks(block_ids(blocks[k]), z, held, rows)
+        place_v[k] = jnp.where(mine & (rank == slot), 1.0, 0.0).astype(BF16)
     for p in range(PIECES):
         relay(1, [p])
         relay(2, [p])
     main(1)
-    relay(3, [0])
+    relay(3, range(PIECES // 2))
     post(0)
-    relay(3, range(1, PIECES))
+    relay(3, range(PIECES // 2, PIECES))
     main(2)
     post(1)
+    target = jnp.zeros((rows, LANES), F32)
+    for o in range(n):
+        mine, rank = owner_ranks(block_ids(z), z * 0 + o, held, rows)
+        target = jnp.where(mine, rank + o * slots, target)
+    wide_slot = lax.broadcasted_iota(jnp.int32, (rows, 2 * LANES), 1).astype(F32)
+    own_place[...] = jnp.where(
+        jnp.concatenate([target, target], axis=1) == wide_slot, 1.0, 0.0
+    ).astype(BF16)
+    post(2)
     main(3)
-    post(2)
     post(3)
 
-    ids = block_ids(z)
-    places = [placement(ids, z * 0 + o, held, rows)[:, :slots] for o in range(n)]
     for k in range(1, n):
-        b = blocks[k]
-        remote(
-            lora_recv.at[b], lora_recv.at[b], lo_ssem.at[k], lo_rsem.at[b], z, t
-        ).wait_recv()
+        dst = lora_recv.at[slot_rows(blocks[k])]
+        remote(dst, dst, lo_ssem.at[k], lo_rsem.at[blocks[k]], z, t).wait_recv()
+    for q in range(n):
+        cs = slice(q * quarter, (q + 1) * quarter)
+        lora_sum[:, cs] = jnp.dot(
+            own_place[:, : n * slots], lora_recv[:, cs], preferred_element_type=F32
+        )
     for src in range(n):
 
         def arrive(src=src):
@@ -459,10 +475,7 @@
 
         pl.when((z - t) * (z - t) + (src - t) * (src - t) > 0)(arrive)
         cs = slice(src * quarter, (src + 1) * quarter)
-        acc = out_recv[src].astype(F32)
-        for o in range(n):
-            acc = acc + jnp.dot(places[o], lora_recv[o, :, cs], preferred_element_type=F32)
-        out_ref[:, cs] = acc.astype(BF16)
+        out_ref[:, cs] = (out_recv[src].astype(F32) + lora_sum[:, cs]).astype(BF16)
 
     for i in range(1, n):
         id_copy(i).wait_send()
@@ -519,8 +532,8 @@
             pltpu.VMEM((rows * span, kv_width), BF16),
             pltpu.VMEM((rows * span, kv_width), BF16),
             pltpu.VMEM(output_weight.shape, BF16),
-            pltpu.VMEM((held, rank_width, width), BF16),
-            pltpu.VMEM(adapter_up.shape, BF16),
+            pltpu.VMEM((held * rank_width, width), BF16),
+            pltpu.VMEM((held * rank_width, width), BF16),
             pltpu.VMEM(token_key.shape, BF16),
             pltpu.VMEM(token_value.shape, BF16),
             pltpu.VMEM((1, rows), jnp.int32),
@@ -534,10 +547,13 @@
             pltpu.VMEM((n, rows, quarter), F32),
             pltpu.VMEM((n, n, rows, quarter), BF16),
             pltpu.VMEM((n, slots, width), BF16),
-            pltpu.VMEM((n, slots, width), BF16),
+            pltpu.VMEM((n * slots, width), BF16),
             pltpu.VMEM((n, rows, quarter), BF16),
             pltpu.VMEM((n, rows, quarter), BF16),
-            dma((14,)),
+            pltpu.VMEM((n, rows, LANES), BF16),
+            pltpu.VMEM((rows, 2 * LANES), BF16),
+            pltpu.VMEM((rows, width), F32),
+            dma((20,)),
             dma((n - 1,)), dma((n,)),
             dma((2, PIECES)), dma((n, PIECES)), dma((n, PIECES)),
             dma((n, n - 1)), dma((n, n)),
@@ -561,8 +577,8 @@
         lengths.reshape(1, rows),
         adapter_index.reshape(1, rows),
         output_weight,
-        adapter_down.transpose(0, 2, 1),
-        adapter_up,
+        adapter_down.transpose(0, 2, 1).reshape(held * rank_width, width),
+        adapter_up.reshape(held * rank_width, width),
     )
 
 

time: 63.6 us -> 61.2 us (0.962)
  Pallas kernels: 61.7 us -> 59.1 us
    pallas_call x1, Pallas kernels: 61.7 us -> 59.1 us  [fused_body(): pl.pallas_call(kernel, out_shape=jax.ShapeDtypeStruct((rows, width), BF16...]
where the time goes in v3:
time: 61.2 us; the launch traced here: 60.9 us
  Pallas kernels  59.1 us (97%)
  local copies, waits for them, and re-layouts  1.77 us (3%)
    pallas_call x1, Pallas kernels, fused_body(): pl.pallas_call(kernel, out_shape=jax.ShapeDtypeStruct((rows, width), BF16...  59.1 us
    unnamed x1, local copies, waits for them, and re-layouts  1.77 us

profile of v3, /device:TPU:0, one launch (start us, length us, event | category | flops | bytes accessed | tf_op | source)
XLA Modules:
  0.0 60.9 jit_solution(12651875797037034856)
XLA Ops:
  0.0 59.1 %shard_map.100 = bf16[96,2048]{1,0:T(8,128)(2,1)} custom-call(bf16[96,2048]{1,0:T(8,128)(2,1)} %q_hbm.1, bf16[6144,256]{1,0:T(8,128)(2,1)} %bitcast.8, bf16[6144,256]{1,0:T(8,128)(2,1)} %bitcast.9, bf16[96,256]{1,0:T(8,128)(2,1)} %tk_hbm.1, bf16[96,256]{1,0:T(8,128)(2,1)} %tv_hbm.1, s32[1,96]{1,0:T(1,128)} %bitcast.12, s32[1,96]{1,0:T(1,128)} %bitcast.13, ...), custom_call_target="tpu_custom_call" | custom-call | flops 3623878656 | bytes 14680064 | tf_op jit(solution)/shard_map/pallas_call | solution.py:525
  59.1 1.8 %copy.12 = bf16[96,2048]{1,0:T(8,128)(2,1)} copy(bf16[96,2048]{1,0:T(8,128)(2,1)} %shard_map.100) | data formatting | bytes 786432

commit v4 on v3

--- a/solution.py
+++ b/solution.py
@@ -192,29 +192,14 @@
             ]
 
 
-def owner_ranks(ids, owner, held, rows):
-    low = (owner * held).astype(F32)
-    mine = (ids >= low) & (ids < low + held)
-    tri = (
-        lax.broadcasted_iota(jnp.int32, (rows, rows), 0)
-        > lax.broadcasted_iota(jnp.int32, (rows, rows), 1)
-    )
-    rank = jnp.dot(
-        jnp.where(tri, 1.0, 0.0).astype(BF16),
-        jnp.where(mine, 1.0, 0.0).astype(BF16),
-        preferred_element_type=F32,
-    )
-    return mine, rank
-
-
 def kernel(
     q_hbm, k_hbm, v_hbm, tk_hbm, tv_hbm, len_hbm, ids_hbm, w_hbm, down_hbm, up_hbm,
     out_ref,
-    q_v, k_v, v_v, w_v, down_v, up_v, tk_ref, tv_ref, len_v, ids_v, len_ref,
+    q_v, k_v, v_v, w_v, down_v, up_v, up_src, tk_ref, tv_ref, len_v, ids_v, len_ref,
     ids_all, attn_all, u_send, u_recv, rs_send, rs_own, rs_recv,
-    lora_send, lora_recv, out_send, out_recv, place_v, own_place, lora_sum,
+    u_all, up_all, out_send, out_recv,
     load_sem, id_ssem, id_rsem, at_ssem, fw_ssem, at_rsem, u_ssem, u_rsem,
-    rs_ssem, rs_rsem, lo_ssem, lo_rsem, out_ssem, out_rsem,
+    rs_ssem, rs_rsem, ua_ssem, ua_rsem, up_ssem, up_rsem, y_ssem, y_rsem, out_ssem, out_rsem,
 ):
     z = lax.axis_index("batch")
     t = lax.axis_index("tensor")
@@ -222,7 +207,8 @@
     n = 4
     held = 4
     rank_width = down_v.shape[0] // held
-    slots = lora_send.shape[1]
+    y = lax.axis_index("groups")
+    share = down_v.shape[0] // 2
     quarter = width // n
     half = rows // 2
     piece = rows // PIECES
@@ -244,6 +230,9 @@
         pltpu.make_async_copy(tk_hbm, tk_ref, load_sem.at[15]),
         pltpu.make_async_copy(tv_hbm, tv_ref, load_sem.at[16]),
     ]
+    pl.semaphore_signal(
+        barrier, inc=1, device_id={"groups": 1 - y}, device_id_type=pl.DeviceIdType.MESH
+    )
     loads = [pltpu.make_async_copy(q_hbm, q_v, load_sem.at[0])]
     for p in range(PIECES):
         part = pl.ds(p * piece * span, piece * span)
@@ -254,7 +243,7 @@
         pltpu.make_async_copy(w_hbm, w_v, load_sem.at[18]),
         pltpu.make_async_copy(up_hbm, up_v, load_sem.at[19]),
     ]
-    for load in small_loads + loads:
+    for load in [tail_loads[2]] + small_loads + loads:
         load.start()
     for load in small_loads:
         load.wait()
@@ -278,7 +267,7 @@
         loads[1 + 2 * p].wait()
         loads[2 + 2 * p].wait()
         if p == 0:
-            for load in tail_loads:
+            for load in tail_loads[:2]:
                 load.start()
 
         def step(i, carry):
@@ -289,9 +278,10 @@
         per = piece // STEP_ROWS
         lax.fori_loop(p * per, (p + 1) * per, step, 0)
         if p == 0:
-            pl.semaphore_wait(barrier, n * n - 1)
+            pl.semaphore_wait(barrier, n * n)
             for i in range(1, n):
                 id_copy(i).start()
+            tail_loads[2].wait()
 
         @pl.when(z < n - 1)
         def _():
@@ -300,19 +290,57 @@
         @pl.when(z > 0)
         def _():
             own_copy(0, p).start()
+
+    def share_rows(owner, group):
+        return pl.ds(pl.multiple_of((owner * 2 + group) * share, share), share)
+
+    def up_copy(i):
+        q = (t + i) % n
+        return remote(
+            up_src.at[q], up_all.at[share_rows(z, y)], up_ssem.at[i], up_rsem.at[z], t, q
+        )
+
+    def cross_copy(owner, group):
+        part = up_all.at[share_rows(owner, group)]
+        return pltpu.make_async_remote_copy(
+            src_ref=part, dst_ref=part, send_sem=y_ssem.at[owner], recv_sem=y_rsem.at[owner],
+            device_id={"groups": 1 - y}, device_id_type=pl.DeviceIdType.MESH,
+        )
+
+    mine_up = pl.ds(pl.multiple_of(y * share, share), share)
+    for q in range(n):
+        up_src[q] = up_v[mine_up, q * quarter : (q + 1) * quarter]
+    for i in range(1, n):
+        up_copy(i).start()
+
+    @pl.when(t != z)
+    def _():
+        up_copy(0).start()
+
+    @pl.when(t == z)
+    def _():
+        up_all[share_rows(z, y), :] = up_src[t]
+
+    def gather_up():
+        for o in range(n):
+            here = (z - t) * (z - t) + (z - o) * (z - o) > 0
+
+            @pl.when(here)
+            def _(o=o):
+                part = up_all.at[share_rows(o, y)]
+                remote(part, part, up_ssem.at[0], up_rsem.at[o], z, t).wait_recv()
+
+            cross_copy(o, y).start()
 
     blocks = [z, z + 1 - 2 * (z % 2), 2 - z // 2, 3 - 3 * (z // 2)]
 
     def block_ids(b):
         return ids_all[b].astype(F32)
 
-    def adapter_mask(ids):
+    def adapter_mask(ids, owner):
         wide = jnp.concatenate([ids, ids], axis=1)
         lane = lax.broadcasted_iota(jnp.int32, wide.shape, 1)
-        return wide == (z * held + lane // rank_width).astype(F32)
-
-    def slot_rows(owner):
-        return pl.ds(pl.multiple_of(owner * slots, slots), slots)
+        return wide == (owner * held + lane // rank_width).astype(F32)
 
     def forward(k, p, to):
         b = blocks[k]
@@ -326,17 +354,17 @@
 
     def rs_copy(k, i):
         return remote(
-            rs_send.at[k, i - 1], rs_recv.at[k, t], rs_ssem.at[k, i - 1], rs_rsem.at[k, t],
+            rs_send.at[k, i - 1], rs_recv.at[blocks[k], t], rs_ssem.at[k, i - 1], rs_rsem.at[blocks[k], t],
             z, (t + i) % n,
         )
 
-    def lora_copy(k):
-        return remote(
-            lora_send.at[k], lora_recv.at[slot_rows(z)], lo_ssem.at[k], lo_rsem.at[z], blocks[k], t
-        )
-
-    def out_copy(k):
-        return remote(out_send.at[k], out_recv.at[t], out_ssem.at[k], out_rsem.at[t], blocks[k], z)
+    def ua_copy(k, i):
+        b = blocks[k]
+        part = u_all.at[b, z]
+        return remote(part, part, ua_ssem.at[k, i - 1], ua_rsem.at[b, z], (z + i) % n, t)
+
+    def out_copy(b):
+        return remote(out_send.at[b], out_recv.at[t], out_ssem.at[b], out_rsem.at[t], b, z)
 
     middle = (z * (n - 1 - z)) > 0
 
@@ -363,7 +391,7 @@
         u = lax.dot_general(
             x, down_v[...], (((1,), (1,)), ((), ())), preferred_element_type=F32
         )
-        u = jnp.where(adapter_mask(ids), u, 0.0)
+        u = jnp.where(adapter_mask(ids, z), u, 0.0)
         u = u[:, :LANES] + u[:, LANES:]
         u = u[:, :rank_width] + u[:, rank_width:]
         u_send[k] = jnp.concatenate([u[:half], u[half:]], axis=1)
@@ -380,7 +408,7 @@
 
         lax.fori_loop(1, n, project, 0)
         cols = pl.ds(pl.multiple_of(t * quarter, quarter), quarter)
-        rs_own[k] = jnp.dot(attn_all[b], w_v[:, cols], preferred_element_type=F32)
+        rs_own[b] = jnp.dot(attn_all[b], w_v[:, cols], preferred_element_type=F32)
 
     def post(k):
         b = blocks[k]
@@ -392,51 +420,50 @@
             ).wait_recv()
             total = total + u_recv[k, src]
         u = jnp.concatenate([total[:, :rank_width], total[:, rank_width:]], axis=0)
-        u = jnp.concatenate([u, u], axis=1)
-        u = jnp.concatenate([u, u], axis=1)
-        u = jnp.where(adapter_mask(block_ids(b)), u, 0.0).astype(BF16)
-        compact = lax.dot_general(
-            place_v[k], u, (((0,), (0,)), ((), ())), preferred_element_type=F32
-        )[:slots].astype(BF16)
-        target = lora_recv.at[slot_rows(z)] if k == 0 else lora_send.at[k]
-        for q in range(n):
-            cs = slice(q * quarter, (q + 1) * quarter)
-            acc = jnp.dot(compact, up_v[:, cs], preferred_element_type=F32)
-            target[:, cs] = (adapter_scale * acc).astype(BF16)
-        if k > 0:
-            lora_copy(k).start()
-
-        sums = rs_own[k]
+        u_all[b, z] = jnp.concatenate([u, u], axis=1).astype(BF16)
+        for i in range(1, n):
+            ua_copy(k, i).start()
+
+    def finish(b):
+        sums = rs_own[b]
         for i in range(1, n):
             src = (t + i) % n
             remote(
-                rs_recv.at[k, src], rs_recv.at[k, src], rs_ssem.at[k, i - 1], rs_rsem.at[k, src],
+                rs_recv.at[b, src], rs_recv.at[b, src], rs_ssem.at[0, i - 1], rs_rsem.at[b, src],
                 z, src,
             ).wait_recv()
-            sums = sums + rs_recv[k, src].astype(F32)
-        out_send[k] = sums.astype(BF16)
-        if k > 0:
-            out_copy(k).start()
-        else:
-
-            @pl.when(t != z)
-            def _():
-                out_copy(0).start()
-
-            @pl.when(t == z)
-            def _():
-                out_recv[t] = out_send[0]
-
-    for load in tail_loads:
+            sums = sums + rs_recv[b, src].astype(F32)
+        for i in range(1, n):
+            o = (z + i) % n
+            part = u_all.at[b, o]
+            remote(part, part, ua_ssem.at[0, i - 1], ua_rsem.at[b, o], o, t).wait_recv()
+        ids = block_ids(b)
+        picked = []
+        for o in range(n):
+            uo = u_all[b, o].astype(F32)
+            uo = jnp.concatenate([uo, uo], axis=1)
+            picked.append(jnp.where(adapter_mask(ids, z * 0 + o), uo, 0.0).astype(BF16))
+        acc = jnp.dot(
+            jnp.concatenate(picked, axis=1), up_all[...], preferred_element_type=F32
+        )
+        lora = (adapter_scale * acc).astype(BF16).astype(F32)
+        out_send[b] = (sums + lora).astype(BF16)
+        away = (b - z) * (b - z) + (t - z) * (t - z) > 0
+
+        @pl.when(away)
+        def _():
+            out_copy(b).start()
+
+        @pl.when(jnp.logical_not(away))
+        def _():
+            out_recv[t] = out_send[b]
+
+    for load in tail_loads[:2]:
         load.wait()
     main(0)
     for k in range(1, n):
         b = blocks[k]
         remote(ids_all.at[b], ids_all.at[b], id_ssem.at[0], id_rsem.at[b], z, t).wait_recv()
-    slot = lax.broadcasted_iota(jnp.int32, (rows, LANES), 1).astype(F32)
-    for k in range(n):
-        mine, rank = owner_ranks(block_ids(blocks[k]), z, held, rows)
-        place_v[k] = jnp.where(mine & (rank == slot), 1.0, 0.0).astype(BF16)
     for p in range(PIECES):
         relay(1, [p])
         relay(2, [p])
@@ -444,28 +471,17 @@
     relay(3, range(PIECES // 2))
     post(0)
     relay(3, range(PIECES // 2, PIECES))
+    post(1)
+    gather_up()
     main(2)
-    post(1)
-    target = jnp.zeros((rows, LANES), F32)
+    post(2)
     for o in range(n):
-        mine, rank = owner_ranks(block_ids(z), z * 0 + o, held, rows)
-        target = jnp.where(mine, rank + o * slots, target)
-    wide_slot = lax.broadcasted_iota(jnp.int32, (rows, 2 * LANES), 1).astype(F32)
-    own_place[...] = jnp.where(
-        jnp.concatenate([target, target], axis=1) == wide_slot, 1.0, 0.0
-    ).astype(BF16)
-    post(2)
+        cross_copy(o, 1 - y).wait_recv()
     main(3)
     post(3)
-
-    for k in range(1, n):
-        dst = lora_recv.at[slot_rows(blocks[k])]
-        remote(dst, dst, lo_ssem.at[k], lo_rsem.at[blocks[k]], z, t).wait_recv()
-    for q in range(n):
-        cs = slice(q * quarter, (q + 1) * quarter)
-        lora_sum[:, cs] = jnp.dot(
-            own_place[:, : n * slots], lora_recv[:, cs], preferred_element_type=F32
-        )
+    for b in (1, 2, 0, 3):
+        finish(b)
+
     for src in range(n):
 
         def arrive(src=src):
@@ -475,7 +491,7 @@
 
         pl.when((z - t) * (z - t) + (src - t) * (src - t) > 0)(arrive)
         cs = slice(src * quarter, (src + 1) * quarter)
-        out_ref[:, cs] = (out_recv[src].astype(F32) + lora_sum[:, cs]).astype(BF16)
+        out_ref[:, cs] = out_recv[src]
 
     for i in range(1, n):
         id_copy(i).wait_send()
@@ -498,14 +514,21 @@
         for i in range(1, n):
             u_copy(k, i).wait_send()
             rs_copy(k, i).wait_send()
-        if k > 0:
-            lora_copy(k).wait_send()
+            ua_copy(k, i).wait_send()
+        away = (k - z) * (k - z) + (t - z) * (t - z) > 0
+
+        @pl.when(away)
+        def _():
             out_copy(k).wait_send()
-        else:
-
-            @pl.when(t != z)
-            def _():
-                out_copy(0).wait_send()
+
+        cross_copy(k, y).wait_send()
+
+    for i in range(1, n):
+        up_copy(i).wait_send()
+
+    @pl.when(t != z)
+    def _():
+        up_copy(0).wait_send()
 
 
 def fused_body(
@@ -516,7 +539,6 @@
     span, kv_width = cached_keys.shape[1:]
     n = lax.axis_size("batch")
     held, _, rank_width = adapter_down.shape
-    slots = max(2, 2 * rows // n)
     quarter = width // n
     vmem = pl.BlockSpec(memory_space=pltpu.VMEM)
     hbm = pl.BlockSpec(memory_space=pl.ANY)
@@ -534,6 +556,7 @@
             pltpu.VMEM(output_weight.shape, BF16),
             pltpu.VMEM((held * rank_width, width), BF16),
             pltpu.VMEM((held * rank_width, width), BF16),
+            pltpu.VMEM((n, held * rank_width // 2, quarter), BF16),
             pltpu.VMEM(token_key.shape, BF16),
             pltpu.VMEM(token_value.shape, BF16),
             pltpu.VMEM((1, rows), jnp.int32),
@@ -546,18 +569,17 @@
             pltpu.VMEM((n, n - 1, rows, quarter), BF16),
             pltpu.VMEM((n, rows, quarter), F32),
             pltpu.VMEM((n, n, rows, quarter), BF16),
-            pltpu.VMEM((n, slots, width), BF16),
-            pltpu.VMEM((n * slots, width), BF16),
+            pltpu.VMEM((n, n, rows, LANES), BF16),
+            pltpu.VMEM((n * held * rank_width, quarter), BF16),
             pltpu.VMEM((n, rows, quarter), BF16),
             pltpu.VMEM((n, rows, quarter), BF16),
-            pltpu.VMEM((n, rows, LANES), BF16),
-            pltpu.VMEM((rows, 2 * LANES), BF16),
-            pltpu.VMEM((rows, width), F32),
             dma((20,)),
             dma((n - 1,)), dma((n,)),
             dma((2, PIECES)), dma((n, PIECES)), dma((n, PIECES)),
             dma((n, n - 1)), dma((n, n)),
             dma((n, n - 1)), dma((n, n)),
+            dma((n, n - 1)), dma((n, n)),
+            dma((n,)), dma((n,)),
             dma((n,)), dma((n,)),
             dma((n,)), dma((n,)),
         ],
@@ -583,7 +605,7 @@
 
 
 def solution(mesh):
-    fused = mesh.shape["batch"] == 4 and mesh.shape["tensor"] == 4
+    fused = mesh.shape["batch"] == 4 and mesh.shape["tensor"] == 4 and mesh.shape["groups"] == 2
     placed = (
         P(("groups", "batch"), "tensor"),
         P(("groups", "batch"), None, "tensor"),

time: 61.2 us -> 83.7 us (1.37)
  the two profiles are of different devices: /device:TPU:0 before, /device:TPU:1 now
where the time goes in v4:
time: 83.7 us; the launch traced here: 83.5 us
  Pallas kernels  81.7 us (98%)
  local copies, waits for them, and re-layouts  1.77 us (2%)
    pallas_call x1, Pallas kernels, fused_body(): pl.pallas_call(kernel, out_shape=jax.ShapeDtypeStruct((rows, width), BF16...  81.7 us
    unnamed x1, local copies, waits for them, and re-layouts  1.77 us

profile of v4, /device:TPU:1, one launch (start us, length us, event | category | flops | bytes accessed | tf_op | source)
XLA Modules:
  0.0 83.5 jit_solution(11816129502252093815)
XLA Ops:
  0.0 81.7 %shard_map.100 = bf16[96,2048]{1,0:T(8,128)(2,1)} custom-call(bf16[96,2048]{1,0:T(8,128)(2,1)} %q_hbm.1, bf16[6144,256]{1,0:T(8,128)(2,1)} %bitcast.8, bf16[6144,256]{1,0:T(8,128)(2,1)} %bitcast.9, bf16[96,256]{1,0:T(8,128)(2,1)} %tk_hbm.1, bf16[96,256]{1,0:T(8,128)(2,1)} %tv_hbm.1, s32[1,96]{1,0:T(1,128)} %bitcast.12, s32[1,96]{1,0:T(1,128)} %bitcast.13, ...), custom_call_target="tpu_custom_call" | custom-call | flops 3623878656 | bytes 14680064 | tf_op jit(solution)/shard_map/pallas_call | solution.py:547
  81.7 1.8 %copy.12 = bf16[96,2048]{1,0:T(8,128)(2,1)} copy(bf16[96,2048]{1,0:T(8,128)(2,1)} %shard_map.100) | data formatting | bytes 786432

commit v5 on v4

--- a/solution.py
+++ b/solution.py
@@ -262,6 +262,22 @@
         to = z + 1 if direction else z - 1
         return remote(part, part, at_ssem.at[direction, p], at_rsem.at[z, p], to, t)
 
+    def share_rows(owner, group):
+        return pl.ds(pl.multiple_of((owner * 2 + group) * share, share), share)
+
+    def up_copy(i):
+        q = (t + i) % n
+        return remote(
+            up_src.at[q], up_all.at[share_rows(z, y)], up_ssem.at[i], up_rsem.at[z], t, q
+        )
+
+    def cross_copy(owner, group):
+        part = up_all.at[share_rows(owner, group)]
+        return pltpu.make_async_remote_copy(
+            src_ref=part, dst_ref=part, send_sem=y_ssem.at[owner], recv_sem=y_rsem.at[owner],
+            device_id={"groups": 1 - y}, device_id_type=pl.DeviceIdType.MESH,
+        )
+
     loads[0].wait()
     for p in range(PIECES):
         loads[1 + 2 * p].wait()
@@ -282,6 +298,20 @@
             for i in range(1, n):
                 id_copy(i).start()
             tail_loads[2].wait()
+            mine_up = pl.ds(pl.multiple_of(y * share, share), share)
+            for q in range(n):
+                up_src[q] = up_v[mine_up, q * quarter : (q + 1) * quarter]
+            for i in range(1, n):
+                up_copy(i).start()
+
+            @pl.when(t != z)
+            def _():
+                up_copy(0).start()
+
+            @pl.when(t == z)
+            def _():
+                up_all[share_rows(z, y), :] = up_src[t]
+
 
         @pl.when(z < n - 1)
         def _():
@@ -290,36 +320,6 @@
         @pl.when(z > 0)
         def _():
             own_copy(0, p).start()
-
-    def share_rows(owner, group):
-        return pl.ds(pl.multiple_of((owner * 2 + group) * share, share), share)
-
-    def up_copy(i):
-        q = (t + i) % n
-        return remote(
-            up_src.at[q], up_all.at[share_rows(z, y)], up_ssem.at[i], up_rsem.at[z], t, q
-        )
-
-    def cross_copy(owner, group):
-        part = up_all.at[share_rows(owner, group)]
-        return pltpu.make_async_remote_copy(
-            src_ref=part, dst_ref=part, send_sem=y_ssem.at[owner], recv_sem=y_rsem.at[owner],
-            device_id={"groups": 1 - y}, device_id_type=pl.DeviceIdType.MESH,
-        )
-
-    mine_up = pl.ds(pl.multiple_of(y * share, share), share)
-    for q in range(n):
-        up_src[q] = up_v[mine_up, q * quarter : (q + 1) * quarter]
-    for i in range(1, n):
-        up_copy(i).start()
-
-    @pl.when(t != z)
-    def _():
-        up_copy(0).start()
-
-    @pl.when(t == z)
-    def _():
-        up_all[share_rows(z, y), :] = up_src[t]
 
     def gather_up():
         for o in range(n):
@@ -477,10 +477,12 @@
     post(2)
     for o in range(n):
         cross_copy(o, 1 - y).wait_recv()
+    finish(1)
+    finish(2)
     main(3)
     post(3)
-    for b in (1, 2, 0, 3):
-        finish(b)
+    finish(0)
+    finish(3)
 
     for src in range(n):
 

time: 83.7 us -> 84.5 us (level)
  no operation moved by 1% of the time
where the time goes in v5:
time: 84.5 us; the launch traced here: 84.3 us
  Pallas kernels  82.5 us (98%)
  local copies, waits for them, and re-layouts  1.77 us (2%)
    pallas_call x1, Pallas kernels, fused_body(): pl.pallas_call(kernel, out_shape=jax.ShapeDtypeStruct((rows, width), BF16...  82.5 us
    unnamed x1, local copies, waits for them, and re-layouts  1.77 us

profile of v5, /device:TPU:1, one launch (start us, length us, event | category | flops | bytes accessed | tf_op | source)
XLA Modules:
  0.0 84.3 jit_solution(9825013049358273535)
XLA Ops:
  0.0 82.5 %shard_map.100 = bf16[96,2048]{1,0:T(8,128)(2,1)} custom-call(bf16[96,2048]{1,0:T(8,128)(2,1)} %q_hbm.1, bf16[6144,256]{1,0:T(8,128)(2,1)} %bitcast.8, bf16[6144,256]{1,0:T(8,128)(2,1)} %bitcast.9, bf16[96,256]{1,0:T(8,128)(2,1)} %tk_hbm.1, bf16[96,256]{1,0:T(8,128)(2,1)} %tv_hbm.1, s32[1,96]{1,0:T(1,128)} %bitcast.12, s32[1,96]{1,0:T(1,128)} %bitcast.13, ...), custom_call_target="tpu_custom_call" | custom-call | flops 3623878656 | bytes 14680064 | tf_op jit(solution)/shard_map/pallas_call | solution.py:549
  82.6 1.8 %copy.12 = bf16[96,2048]{1,0:T(8,128)(2,1)} copy(bf16[96,2048]{1,0:T(8,128)(2,1)} %shard_map.100) | data formatting | bytes 786432
